TPU v7x, 32 devices: a whole 2x2x4 slice. The times are simulated.
32 devices in a mesh: seq: 8 (over z, x), ch: 4 (over y, core).
Axes of the slice: x: 2, y: 2, z: 4, core: 2. Of those that a mesh axis runs over, the one named last changes fastest.
Arguments:
- q_in: bfloat16 [4096, 4096], P('seq', 'ch'), may hold values from -6 to 6
- k_in: bfloat16 [4096, 4096], P('seq', 'ch'), may hold values from -6 to 6
- v_in: bfloat16 [4096, 4096], P('seq', 'ch'), may hold values from -6 to 6
- conv_weight: float32 [3, 7, 4096], P(None, None, 'ch'), may hold values from -2 to 2
- mode_residue: float32 [16, 4096], P(None, 'ch'), may hold values from -3 to 3
- decay_rate: float32 [16, 4096], P(None, 'ch'), may hold values from 0.00012207031 to 0.04
- skip_gain: float32 [4096], P('ch'), may hold values from -4 to 4
- tenant_ids: int32 [32], P('seq'), may hold values from 0 to 7
- valid_length: int32 [1], replicated, may hold values from 3840 to 4096
- reft_proj: bfloat16 [8, 4, 4096], P(None, None, 'ch'), may hold values from -0.25 to 0.25
- reft_weight: bfloat16 [8, 4, 4096], P(None, None, 'ch'), may hold values from -0.25 to 0.25
- reft_bias: float32 [8, 4], replicated, may hold values from -8 to 8
Outputs:
- edited: bfloat16 [4096, 4096], P('seq', 'ch')
Inputs may be any that keep to these rules, and one draw needn't show every extreme that they name: `tenant_ids`: the tenant of the positions t * 128 to (t + 1) * 128 - 1. Positions from valid_length on are padding.
All inputs are finite; a program needn't handle non-finite values.
Results may differ from a plain program's by a relative error of at most 0.001.
Values may be sent and summed in bfloat16 or wider, within the bound.
A program may use at most 128 MiB of HBM per device.

v0:
```python
import functools

import jax
import jax.numpy as jnp
from jax import lax
from jax.experimental import pallas as pl
from jax.experimental.pallas import tpu as pltpu
from jax.sharding import PartitionSpec as P

LANES = 128
UNROLL = 8
PAD = 8
HALO = 16
F32 = jnp.float32
BF16 = jnp.bfloat16


def spread(src, dst, start, limit):
    rows, width = src.shape
    step = min(64, rows)

    def body(block, carry):
        first = pl.multiple_of(block * step, step)
        row = first + lax.broadcasted_iota(jnp.int32, (step, LANES), 0)
        for group in range(width // LANES):
            value = src[pl.ds(first, step), group * LANES : (group + 1) * LANES].astype(F32)
            dst[pl.ds(start + first, step), group, :] = jnp.where(row < limit, value, 0.0)
        return carry

    lax.fori_loop(0, rows // step, body, 0)


def spread_small(src, dst, start):
    rows, width = src.shape
    for group in range(width // LANES):
        dst[start : start + rows, group, :] = src[:, group * LANES : (group + 1) * LANES]


def short_block(ref, taps, base, reach, first):
    window = [ref[first + PAD - reach + 1 + i] for i in range(UNROLL + reach - 1)]
    total = [None] * UNROLL
    for offset in range(reach):
        weight = taps[base + offset]
        for i in range(UNROLL):
            term = weight * window[i + reach - 1 - offset]
            total[i] = term if total[i] is None else total[i] + term
    return total


def scan_kernel(
    valid_ref, q_ref, k_ref, v_ref, halo_ref, taps_ref, residue_ref, rate_ref, gain_ref,
    partial_ref, query_ref, final_ref, q_rows, k_rows, v_rows, taps, decay, scale,
):
    rows, width = q_ref.shape
    reach = taps_ref.shape[1]
    modes = rate_ref.shape[0]
    limit = valid_ref[0] - lax.axis_index("seq") * rows
    for i, (ref, dst) in enumerate(((q_ref, q_rows), (k_ref, k_rows), (v_ref, v_rows))):
        spread(ref, dst, PAD, limit)
        row = lax.broadcasted_iota(jnp.int32, (PAD, LANES), 0) - PAD
        for group in range(width // LANES):
            piece = halo_ref[i, :, group * LANES : (group + 1) * LANES].astype(F32)[HALO - PAD :]
            dst[0:PAD, group, :] = jnp.where(row < limit, piece, 0.0)
        spread_small(taps_ref.at[i], taps, i * reach)
    spread_small(rate_ref, decay, 0)
    spread_small(residue_ref, scale, 0)
    rates = decay[...]
    scale[...] = scale[...] * jnp.sqrt(2.0 * rates)
    decay[...] = jnp.exp(-rates)
    gain = gain_ref[...]

    def body(block, states):
        first = block * UNROLL
        keyed = short_block(k_rows, taps, reach, reach, first)
        valued = short_block(v_rows, taps, 2 * reach, reach, first)
        driven = [a * b for a, b in zip(keyed, valued)]
        query = short_block(q_rows, taps, 0, reach, first)
        for i in range(UNROLL):
            query_ref[first + i] = query[i]
        total = [gain * x for x in driven]
        after = []
        for n in range(modes):
            state, d, a = states[n], decay[n], scale[n]
            for i in range(UNROLL):
                state = d * state + driven[i]
                total[i] = total[i] + a * state
            after.append(state)
        for i in range(UNROLL):
            partial_ref[first + i] = total[i]
        return tuple(after)

    zero = jnp.zeros((width // LANES, LANES), F32)
    states = lax.fori_loop(0, rows // UNROLL, body, (zero,) * modes)
    for n in range(modes):
        final_ref[n] = states[n]


def gate_kernel(
    tenant_ref, partial_ref, query_ref, carry_ref, residue_ref, rate_ref, proj_ref, weight_ref,
    gated_ref, sums_ref, mixed, decay, scale, maps,
):
    rows, width = gated_ref.shape
    modes = rate_ref.shape[0]
    spans = tenant_ref.shape[0]
    span = rows // spans
    rank = proj_ref.shape[1]
    spread_small(rate_ref, decay, 0)
    spread_small(residue_ref, scale, 0)
    rates = decay[...]
    decay[...] = jnp.exp(-rates)
    scale[...] = scale[...] * jnp.sqrt(2.0 * rates) * decay[...] * carry_ref[...]

    def body(block, states):
        first = block * UNROLL
        total = [partial_ref[first + i] for i in range(UNROLL)]
        after = []
        for n in range(modes):
            state, d = states[n], decay[n]
            for i in range(UNROLL):
                total[i] = total[i] + state
                state = state * d
            after.append(state)
        for i in range(UNROLL):
            mixed[first + i] = total[i] * query_ref[first + i]
        return tuple(after)

    lax.fori_loop(0, rows // UNROLL, body, tuple(scale[n] for n in range(modes)))

    def gather(block, carry):
        first = pl.multiple_of(block * 64, 64)
        for group in range(width // LANES):
            gated_ref[pl.ds(first, 64), group * LANES : (group + 1) * LANES] = mixed[
                pl.ds(first, 64), group, :
            ]
        return carry

    lax.fori_loop(0, rows // 64, gather, 0)
    for s in range(spans):
        tenant = tenant_ref[s]
        maps[0:rank, :] = proj_ref[tenant].astype(F32)
        maps[rank : 2 * rank, :] = weight_ref[tenant].astype(F32)
        both = maps[...].astype(BF16)
        value = gated_ref[s * span : (s + 1) * span, :]
        high = value.astype(BF16)
        low = (value - high.astype(F32)).astype(BF16)
        dims = (((1,), (1,)), ((), ()))
        sums_ref[:, s * span : (s + 1) * span] = lax.dot_general(
            both, high, dims, preferred_element_type=F32
        ) + lax.dot_general(both, low, dims, preferred_element_type=F32)


def edit_kernel(tenant_ref, valid_ref, bias_ref, gated_ref, sums_ref, proj_ref, out_ref, maps):
    rows, width = gated_ref.shape
    spans = tenant_ref.shape[0]
    span = rows // spans
    rank = proj_ref.shape[1]
    limit = valid_ref[0] - lax.axis_index("seq") * rows
    line = lax.broadcasted_iota(jnp.int32, (2 * rank, span), 0)
    for s in range(spans):
        tenant = tenant_ref[s]
        maps[0:rank, :] = proj_ref[tenant].astype(F32)
        maps[rank : 2 * rank, :] = proj_ref[tenant].astype(F32)
        totals = sums_ref[:, s * span : (s + 1) * span]
        bias = jnp.zeros((2 * rank, span), F32)
        for r in range(rank):
            bias = jnp.where(line % rank == r, bias_ref[tenant, r], bias)
        change = pltpu.roll(totals, rank, 0) - totals
        delta = jnp.where(line < rank, change, -change) + bias
        high = delta.astype(BF16).astype(F32)
        parts = jnp.where(line < rank, high, delta - high).astype(BF16)
        edit = lax.dot_general(
            parts, maps[...].astype(BF16), (((0,), (0,)), ((), ())), preferred_element_type=F32
        )
        row = s * span + lax.broadcasted_iota(jnp.int32, (span, width), 0)
        value = gated_ref[s * span : (s + 1) * span, :] + edit
        out_ref[s * span : (s + 1) * span, :] = jnp.where(row < limit, value, 0.0).astype(BF16)


def shifted(value, axis, steps):
    count = lax.axis_size(axis)
    return lax.ppermute(value, axis, [(i, i + steps) for i in range(count - steps)])


VMEM = pl.BlockSpec(memory_space=pltpu.VMEM)
SMEM = pl.BlockSpec(memory_space=pltpu.SMEM)


def local(
    q_in, k_in, v_in, conv_weight, mode_residue, decay_rate, skip_gain, tenant_ids, valid_length,
    reft_proj, reft_weight, reft_bias,
):
    rows, width = q_in.shape
    groups = width // LANES
    modes = decay_rate.shape[0]
    reach = conv_weight.shape[1]
    rank = reft_bias.shape[1]
    count = lax.axis_size("seq")
    params = pltpu.CompilerParams(vmem_limit_bytes=48 * 2**20)
    halo = shifted(jnp.stack([x[rows - HALO :] for x in (q_in, k_in, v_in)]), "seq", 1)
    tall = pltpu.VMEM((rows + PAD, groups, LANES), F32)
    small = pltpu.VMEM((modes, groups, LANES), F32)
    cube = jax.ShapeDtypeStruct((rows, groups, LANES), F32)
    partial, query, final = pl.pallas_call(
        scan_kernel,
        out_shape=(cube, cube, jax.ShapeDtypeStruct((modes, groups, LANES), F32)),
        in_specs=[SMEM] + [VMEM] * 8,
        out_specs=(VMEM,) * 3,
        scratch_shapes=[tall, tall, tall, pltpu.VMEM((3 * reach, groups, LANES), F32), small, small],
        compiler_params=params,
    )(
        valid_length, q_in, k_in, v_in, halo, conv_weight, mode_residue, decay_rate,
        skip_gain.reshape(groups, LANES),
    )
    rates = decay_rate.reshape(modes, groups, LANES)
    carry = shifted(final, "seq", 1)
    step = 1
    while step < count:
        carry = carry + jnp.exp(-float(step * rows) * rates) * shifted(carry, "seq", step)
        step *= 2
    gated, sums = pl.pallas_call(
        gate_kernel,
        out_shape=(
            jax.ShapeDtypeStruct((rows, width), F32),
            jax.ShapeDtypeStruct((2 * rank, rows), F32),
        ),
        in_specs=[SMEM] + [VMEM] * 7,
        out_specs=(VMEM,) * 2,
        scratch_shapes=[
            pltpu.VMEM((rows, groups, LANES), F32), small, small, pltpu.VMEM((2 * rank, width), F32),
        ],
        compiler_params=params,
    )(tenant_ids, partial, query, carry, mode_residue, decay_rate, reft_proj, reft_weight)
    totals = lax.psum(sums, "ch")
    return pl.pallas_call(
        edit_kernel,
        out_shape=jax.ShapeDtypeStruct((rows, width), BF16),
        in_specs=[SMEM] * 3 + [VMEM] * 3,
        out_specs=VMEM,
        scratch_shapes=[pltpu.VMEM((2 * rank, width), F32)],
        compiler_params=params,
    )(tenant_ids, valid_length, reft_bias, gated, totals, reft_proj)


def solution(mesh):
    return jax.shard_map(
        local,
        mesh=mesh,
        in_specs=(
            P("seq", "ch"),
            P("seq", "ch"),
            P("seq", "ch"),
            P(None, None, "ch"),
            P(None, "ch"),
            P(None, "ch"),
            P("ch"),
            P("seq"),
            P(),
            P(None, None, "ch"),
            P(None, None, "ch"),
            P(),
        ),
        out_specs=P("seq", "ch"),
        check_vma=False,
    )
```

profile of v0, /device:TPU:0, one launch (start us, length us, event | category | flops | bytes accessed | tf_op | source)
XLA Modules:
  0.0 79.3 jit_solution(9657580546891251846)
XLA Ops:
  0.0 0.8 slice_bitcast_fusion.2
  0.8 0.8 slice_bitcast_fusion
  1.6 4.8 %collective-permute-start = (bf16[3,16,1024]{2,1,0:T(8,128)(2,1)S(1)}, bf16[3,16,1024]{2,1,0:T(8,128)(2,1)S(1)}, u32[]{:S(2)}, u32[]{:S(2)}) collective-permute-start(bf16[3,16,1024]{2,1,0:T(8,128)(2,1)S(1)} %pad_maximum_fusion), channel_id=1, source_target_pairs={{0,4},{4,8},{8,12},{12,16},{16,20},{20,24},{24,28},{1,5},{5,9},{9,... | collective-permute-start | bytes 294920 | tf_op jit(solution)/shard_map/ppermute | solution.py:181
  7.1 1.5 %collective-permute-done.halo_ref = bf16[3,16,1024]{2,1,0:T(8,128)(2,1)S(1)} collective-permute-done((bf16[3,16,1024]{2,1,0:T(8,128)(2,1)S(1)}, bf16[3,16,1024]{2,1,0:T(8,128)(2,1)S(1)}, u32[]{:S(2)}, u32[]{:S(2)}) %collective-permute-start) | collective-permute-done | bytes 98336 | tf_op jit(solution)/shard_map/ppermute | solution.py:181
  8.6 0.0 copy-start.2
  8.6 1.2 %copy-done.2 = bf16[512,1024]{1,0:T(8,128)(2,1)S(1)} copy-done((bf16[512,1024]{1,0:T(8,128)(2,1)S(1)}, bf16[512,1024]{1,0:T(8,128)(2,1)}, u32[]{:S(2)}) %copy-start.2) | copy-done | bytes 1048600
  9.8 0.0 copy-start.3
  9.8 1.2 %copy-done.3 = bf16[512,1024]{1,0:T(8,128)(2,1)S(1)} copy-done((bf16[512,1024]{1,0:T(8,128)(2,1)S(1)}, bf16[512,1024]{1,0:T(8,128)(2,1)}, u32[]{:S(2)}) %copy-start.3) | copy-done | bytes 1048600
  11.1 0.0 copy-start.4
  11.1 1.2 %copy-done.4 = bf16[512,1024]{1,0:T(8,128)(2,1)S(1)} copy-done((bf16[512,1024]{1,0:T(8,128)(2,1)S(1)}, bf16[512,1024]{1,0:T(8,128)(2,1)}, u32[]{:S(2)}) %copy-start.4) | copy-done | bytes 1048600
  12.3 0.0 copy-start.5
  12.3 0.8 %copy-done.5 = f32[16,1024]{1,0:T(8,128)S(1)} copy-done((f32[16,1024]{1,0:T(8,128)S(1)}, f32[16,1024]{1,0:T(8,128)}, u32[]{:S(2)}) %copy-start.5) | copy-done | bytes 65560
  13.1 0.0 copy-start.7
  13.1 0.8 %copy-done.7 = f32[16,1024]{1,0:T(8,128)S(1)} copy-done((f32[16,1024]{1,0:T(8,128)S(1)}, f32[16,1024]{1,0:T(8,128)}, u32[]{:S(2)}) %copy-start.7) | copy-done | bytes 65560
  14.0 0.0 copy-start.10
  14.0 0.9 %copy-done.10 = f32[3,7,1024]{2,1,0:T(8,128)S(1)} copy-done((f32[3,7,1024]{2,1,0:T(8,128)S(1)}, f32[3,7,1024]{2,1,0:T(8,128)}, u32[]{:S(2)}) %copy-start.10) | copy-done | bytes 86040
  14.9 0.0 copy-start.12
  14.9 0.7 copy-done.12
  15.5 0.0 copy-start.14
  15.5 0.0 copy-start.6
  15.5 0.0 copy-start.8
  15.5 0.0 copy-start.9
  15.6 0.0 copy-start.11
  15.6 0.0 copy-start.13
  15.6 13.5 %shard_map.118 = (f32[512,8,128]{2,1,0:T(8,128)S(1)}, f32[512,8,128]{2,1,0:T(8,128)}, f32[16,8,128]{2,1,0:T(8,128)S(1)}) custom-call(s32[1]{0:T(128)S(6)} %copy.17.valid_ref, bf16[512,1024]{1,0:T(8,128)(2,1)S(1)} %copy-done.2, bf16[512,1024]{1,0:T(8,128)(2,1)S(1)} %copy-done.3, bf16[512,1024]{1,0:T(8,128)(2,1)S(1)} %copy-done.4, ...), custom_call_target="tpu_custom_call" | custom-call | tf_op jit(solution)/shard_map/pallas_call | solution.py:203
  29.1 4.3 %collective-permute-start.1 = (f32[16,8,128]{2,1,0:T(8,128)S(1)}, f32[16,8,128]{2,1,0:T(8,128)S(1)}, u32[]{:S(2)}, u32[]{:S(2)}) collective-permute-start(f32[16,8,128]{2,1,0:T(8,128)S(1)} %get-tuple-element.12), channel_id=1, source_target_pairs={{0,4},{4,8},{8,12},{12,16},{16,20},{20,24},{24,28},{1,5},{5,9},{9,... | collective-permute-start | bytes 196616 | tf_op jit(solution)/shard_map/ppermute | solution.py:181
  33.4 1.9 %collective-permute-done.1 = f32[16,8,128]{2,1,0:T(8,128)S(1)} collective-permute-done((f32[16,8,128]{2,1,0:T(8,128)S(1)}, f32[16,8,128]{2,1,0:T(8,128)S(1)}, u32[]{:S(2)}, u32[]{:S(2)}) %collective-permute-start.1) | collective-permute-done | bytes 65568 | tf_op jit(solution)/shard_map/ppermute | solution.py:181
  35.3 4.3 %collective-permute-start.2 = (f32[16,8,128]{2,1,0:T(8,128)S(1)}, f32[16,8,128]{2,1,0:T(8,128)S(1)}, u32[]{:S(2)}, u32[]{:S(2)}) collective-permute-start(f32[16,8,128]{2,1,0:T(8,128)S(1)} %collective-permute-done.1), channel_id=1, source_target_pairs={{0,4},{4,8},{8,12},{12,16},{16,20},{20,24},{24,28},{1,5},{5,9},{9,... | collective-permute-start | bytes 196616 | tf_op jit(solution)/shard_map/ppermute | solution.py:181
  39.7 1.8 %collective-permute-done.2 = f32[16,8,128]{2,1,0:T(8,128)S(1)} collective-permute-done((f32[16,8,128]{2,1,0:T(8,128)S(1)}, f32[16,8,128]{2,1,0:T(8,128)S(1)}, u32[]{:S(2)}, u32[]{:S(2)}) %collective-permute-start.2) | collective-permute-done | bytes 65568 | tf_op jit(solution)/shard_map/ppermute | solution.py:181
  41.5 7.0 %collective-permute-start.3 = (f32[16,8,128]{2,1,0:T(8,128)S(1)}, f32[16,8,128]{2,1,0:T(8,128)S(1)}, u32[]{:S(2)}, u32[]{:S(2)}) collective-permute-start(f32[16,8,128]{2,1,0:T(8,128)S(1)} %fusion.2), channel_id=1, source_target_pairs={{0,8},{4,12},{8,16},{12,20},{16,24},{20,28},{1,9},{5,13},{9,17},{1... | collective-permute-start | bytes 196616 | tf_op jit(solution)/shard_map/ppermute | solution.py:181
  48.5 1.9 %collective-permute-done.3 = f32[16,8,128]{2,1,0:T(8,128)S(1)} collective-permute-done((f32[16,8,128]{2,1,0:T(8,128)S(1)}, f32[16,8,128]{2,1,0:T(8,128)S(1)}, u32[]{:S(2)}, u32[]{:S(2)}) %collective-permute-start.3) | collective-permute-done | bytes 65568 | tf_op jit(solution)/shard_map/ppermute | solution.py:181
  50.4 5.3 %collective-permute-start.4 = (f32[16,8,128]{2,1,0:T(8,128)S(1)}, f32[16,8,128]{2,1,0:T(8,128)S(1)}, u32[]{:S(2)}, u32[]{:S(2)}) collective-permute-start(f32[16,8,128]{2,1,0:T(8,128)S(1)} %fusion.1), channel_id=1, source_target_pairs={{0,16},{4,20},{8,24},{12,28},{1,17},{5,21},{9,25},{13,29},{2,18},{... | collective-permute-start | bytes 196616 | tf_op jit(solution)/shard_map/ppermute | solution.py:181
  55.7 0.0 copy-done.14
  55.7 0.1 copy.13.bias_ref
  55.8 1.8 %collective-permute-done.4 = f32[16,8,128]{2,1,0:T(8,128)S(1)} collective-permute-done((f32[16,8,128]{2,1,0:T(8,128)S(1)}, f32[16,8,128]{2,1,0:T(8,128)S(1)}, u32[]{:S(2)}, u32[]{:S(2)}) %collective-permute-start.4) | collective-permute-done | bytes 65568 | tf_op jit(solution)/shard_map/ppermute | solution.py:181
  57.6 0.0 copy-done.6
  57.6 0.0 copy-done.8
  57.6 0.0 copy-done.9
  57.6 0.0 copy-done.11
  57.6 0.0 copy-done.13
  57.6 6.6 %shard_map.119 = (f32[512,1024]{1,0:T(8,128)S(1)}, f32[8,512]{1,0:T(8,128)S(1)}) custom-call(s32[4]{0:T(128)S(1)} %copy-done.13, f32[512,8,128]{2,1,0:T(8,128)S(1)} %get-tuple-element.10.partial_ref, f32[512,8,128]{2,1,0:T(8,128)} %get-tuple-element.11.query_ref, f32[16,8,128]{2,1,0:T(8,128)S(1)} %fusion.carry_ref, f32[16,1024]{1,0:T(8,128)S(1)} %copy-done.8, ...), custom_call_target="tpu_custom_call" | custom-call | tf_op jit(solution)/shard_map/pallas_call | solution.py:220
  64.2 0.0 copy-start
  64.2 1.3 %copy-done = f32[512,1024]{1,0:T(8,128)} copy-done((f32[512,1024]{1,0:T(8,128)}, f32[512,1024]{1,0:T(8,128)S(1)}, u32[]{:S(2)}) %copy-start) | copy-done | bytes 2097176
  65.5 10.1 %psum.7.sums_ref = f32[8,512]{1,0:T(8,128)S(1)} all-reduce(f32[8,512]{1,0:T(8,128)S(1)} %get-tuple-element.14), channel_id=1, replica_groups=mesh['seq'=8,'ch'=4] {'ch'}, use_global_device_ids=true, to_apply=%region_0.0 | all-reduce | flops 4096 | bytes 32768 | tf_op jit(solution)/shard_map/psum | solution.py:233
  75.6 0.0 copy-start.1
  75.6 1.6 %copy-done.1 = f32[512,1024]{1,0:T(8,128)S(1)} copy-done((f32[512,1024]{1,0:T(8,128)S(1)}, f32[512,1024]{1,0:T(8,128)}, u32[]{:S(2)}) %copy-start.1) | copy-done | bytes 2097176
  77.2 2.0 %shard_map.120 = bf16[512,1024]{1,0:T(8,128)(2,1)} custom-call(s32[4]{0:T(128)S(1)} %copy-done.13, s32[1]{0:T(128)S(6)} %copy.17.valid_ref, f32[8,4]{1,0:T(8,128)S(1)} %copy.13.bias_ref, f32[512,1024]{1,0:T(8,128)S(1)} %copy-done.1, f32[8,512]{1,0:T(8,128)S(1)} %psum.7.sums_ref, bf16[8,4,1024]{2,1,0:T(4,128)(2,1)S(1)} %copy-done.9), custom_call_target="tpu_custom_call" | custom-call | tf_op jit(solution)/shard_map/pallas_call | solution.py:234
  (8 shorter events, 0.1 us)
Async XLA Ops:
  1.6 7.0 %collective-permute-start = (bf16[3,16,1024]{2,1,0:T(8,128)(2,1)S(1)}, bf16[3,16,1024]{2,1,0:T(8,128)(2,1)S(1)}, u32[]{:S(2)}, u32[]{:S(2)}) collective-permute-start(bf16[3,16,1024]{2,1,0:T(8,128)(2,1)S(1)} %pad_maximum_fusion), channel_id=1, source_target_pairs={{0,4},{4,8},{8,12},{12,16},{16,20},{20,24},{24,28},{1,5},{5,9},{9,... | collective-permute-start | bytes 294920 | tf_op jit(solution)/shard_map/ppermute | solution.py:181
  8.6 1.2 %copy-start.2 = (bf16[512,1024]{1,0:T(8,128)(2,1)S(1)}, bf16[512,1024]{1,0:T(8,128)(2,1)}, u32[]{:S(2)}) copy-start(bf16[512,1024]{1,0:T(8,128)(2,1)} %q_ref.1) | copy-start | bytes 3145732
  9.8 1.2 %copy-start.3 = (bf16[512,1024]{1,0:T(8,128)(2,1)S(1)}, bf16[512,1024]{1,0:T(8,128)(2,1)}, u32[]{:S(2)}) copy-start(bf16[512,1024]{1,0:T(8,128)(2,1)} %k_ref.1) | copy-start | bytes 3145732
  11.1 1.2 %copy-start.4 = (bf16[512,1024]{1,0:T(8,128)(2,1)S(1)}, bf16[512,1024]{1,0:T(8,128)(2,1)}, u32[]{:S(2)}) copy-start(bf16[512,1024]{1,0:T(8,128)(2,1)} %v_ref.1) | copy-start | bytes 3145732
  12.3 0.8 %copy-start.5 = (f32[16,1024]{1,0:T(8,128)S(1)}, f32[16,1024]{1,0:T(8,128)}, u32[]{:S(2)}) copy-start(f32[16,1024]{1,0:T(8,128)} %rate_ref.3) | copy-start | bytes 196612
  13.1 0.8 %copy-start.7 = (f32[16,1024]{1,0:T(8,128)S(1)}, f32[16,1024]{1,0:T(8,128)}, u32[]{:S(2)}) copy-start(f32[16,1024]{1,0:T(8,128)} %residue_ref.3) | copy-start | bytes 196612
  14.0 0.9 %copy-start.10 = (f32[3,7,1024]{2,1,0:T(8,128)S(1)}, f32[3,7,1024]{2,1,0:T(8,128)}, u32[]{:S(2)}) copy-start(f32[3,7,1024]{2,1,0:T(8,128)} %taps_ref.1) | copy-start | bytes 258052
  14.9 0.7 copy-start.12
  15.5 40.1 %copy-start.14 = (f32[8,4]{0,1:T(4,128)S(1)}, f32[8,4]{0,1:T(4,128)}, u32[]{:S(2)}) copy-start(f32[8,4]{0,1:T(4,128)} %param.23) | copy-start | bytes 388
  15.5 42.0 %copy-start.6 = (f32[16,1024]{1,0:T(8,128)S(1)}, f32[16,1024]{1,0:T(8,128)}, u32[]{:S(2)}) copy-start(f32[16,1024]{1,0:T(8,128)} %rate_ref.3) | copy-start | bytes 196612
  15.5 42.0 %copy-start.8 = (f32[16,1024]{1,0:T(8,128)S(1)}, f32[16,1024]{1,0:T(8,128)}, u32[]{:S(2)}) copy-start(f32[16,1024]{1,0:T(8,128)} %residue_ref.3) | copy-start | bytes 196612
  15.5 42.0 %copy-start.9 = (bf16[8,4,1024]{2,1,0:T(4,128)(2,1)S(1)}, bf16[8,4,1024]{2,1,0:T(4,128)(2,1)}, u32[]{:S(2)}) copy-start(bf16[8,4,1024]{2,1,0:T(4,128)(2,1)} %proj_ref.3) | copy-start | bytes 196612
  15.6 42.0 %copy-start.11 = (bf16[8,4,1024]{2,1,0:T(4,128)(2,1)S(1)}, bf16[8,4,1024]{2,1,0:T(4,128)(2,1)}, u32[]{:S(2)}) copy-start(bf16[8,4,1024]{2,1,0:T(4,128)(2,1)} %weight_ref.1) | copy-start | bytes 196612
  15.6 42.0 %copy-start.13 = (s32[4]{0:T(128)S(1)}, s32[4]{0:T(128)}, u32[]{:S(2)}) copy-start(s32[4]{0:T(128)} %tenant_ref.3) | copy-start | bytes 52
  29.1 6.2 %collective-permute-start.1 = (f32[16,8,128]{2,1,0:T(8,128)S(1)}, f32[16,8,128]{2,1,0:T(8,128)S(1)}, u32[]{:S(2)}, u32[]{:S(2)}) collective-permute-start(f32[16,8,128]{2,1,0:T(8,128)S(1)} %get-tuple-element.12), channel_id=1, source_target_pairs={{0,4},{4,8},{8,12},{12,16},{16,20},{20,24},{24,28},{1,5},{5,9},{9,... | collective-permute-start | bytes 196616 | tf_op jit(solution)/shard_map/ppermute | solution.py:181
  35.3 6.2 %collective-permute-start.2 = (f32[16,8,128]{2,1,0:T(8,128)S(1)}, f32[16,8,128]{2,1,0:T(8,128)S(1)}, u32[]{:S(2)}, u32[]{:S(2)}) collective-permute-start(f32[16,8,128]{2,1,0:T(8,128)S(1)} %collective-permute-done.1), channel_id=1, source_target_pairs={{0,4},{4,8},{8,12},{12,16},{16,20},{20,24},{24,28},{1,5},{5,9},{9,... | collective-permute-start | bytes 196616 | tf_op jit(solution)/shard_map/ppermute | solution.py:181
  41.5 8.9 %collective-permute-start.3 = (f32[16,8,128]{2,1,0:T(8,128)S(1)}, f32[16,8,128]{2,1,0:T(8,128)S(1)}, u32[]{:S(2)}, u32[]{:S(2)}) collective-permute-start(f32[16,8,128]{2,1,0:T(8,128)S(1)} %fusion.2), channel_id=1, source_target_pairs={{0,8},{4,12},{8,16},{12,20},{16,24},{20,28},{1,9},{5,13},{9,17},{1... | collective-permute-start | bytes 196616 | tf_op jit(solution)/shard_map/ppermute | solution.py:181
  50.4 7.2 %collective-permute-start.4 = (f32[16,8,128]{2,1,0:T(8,128)S(1)}, f32[16,8,128]{2,1,0:T(8,128)S(1)}, u32[]{:S(2)}, u32[]{:S(2)}) collective-permute-start(f32[16,8,128]{2,1,0:T(8,128)S(1)} %fusion.1), channel_id=1, source_target_pairs={{0,16},{4,20},{8,24},{12,28},{1,17},{5,21},{9,25},{13,29},{2,18},{... | collective-permute-start | bytes 196616 | tf_op jit(solution)/shard_map/ppermute | solution.py:181
  64.2 1.3 %copy-start = (f32[512,1024]{1,0:T(8,128)}, f32[512,1024]{1,0:T(8,128)S(1)}, u32[]{:S(2)}) copy-start(f32[512,1024]{1,0:T(8,128)S(1)} %get-tuple-element.13.gated_ref) | copy-start | bytes 6291460
  75.6 1.6 %copy-start.1 = (f32[512,1024]{1,0:T(8,128)S(1)}, f32[512,1024]{1,0:T(8,128)}, u32[]{:S(2)}) copy-start(f32[512,1024]{1,0:T(8,128)} %copy-done) | copy-start | bytes 6291460
where the time goes:
time: 80 us; the launch traced here: 79.3 us
  starting transfers between devices  25.7 us (32%)
  Pallas kernels  22.1 us (28%)
  local copies, waits for them, and re-layouts  11.6 us (14%)
  blocking collectives  10.1 us (13%)
  waiting for transfers between devices  8.88 us (11%)
  between operations  0.81 us (1%)
    ppermute x5, starting transfers between devices, shifted(): lax.ppermute(value, axis, [(i, i + steps) for i in range(count - steps)])  25.7 us
    pallas_call x1, Pallas kernels, local(): pl.pallas_call(scan_kernel, out_shape=(cube, cube, jax.ShapeDtypeStruct((...  13.5 us
    psum x1, blocking collectives, local(): totals = lax.psum(sums, 'ch')  10.1 us
    unnamed x34, local copies, waits for them, and re-layouts  10 us
    ppermute x5, waiting for transfers between devices, shifted(): lax.ppermute(value, axis, [(i, i + steps) for i in range(count - steps)])  8.88 us
    pallas_call x1, Pallas kernels, local(): pl.pallas_call(gate_kernel, out_shape=(jax.ShapeDtypeStruct((rows, width)...  6.56 us
    pallas_call x1, Pallas kernels, local(): pl.pallas_call(edit_kernel, out_shape=jax.ShapeDtypeStruct((rows, width),...  2.05 us
  transfers between devices with their start and end apart: 5, of which 5 were waited for; matrix products, arithmetic and copies ran while one was open for 0% of the time, Pallas kernels for 0%

commit v1 on v0

v1 whole, which is shorter than its diff:
```python
import functools

import jax
import jax.numpy as jnp
from jax import lax
from jax.experimental import pallas as pl
from jax.experimental.pallas import tpu as pltpu
from jax.sharding import PartitionSpec as P

LANES = 128
UNROLL = 8
PAD = 8
HALO = 16
F32 = jnp.float32
BF16 = jnp.bfloat16


def spread(src, dst, start, limit):
    rows, width = src.shape
    step = min(64, rows)

    def body(block, carry):
        first = pl.multiple_of(block * step, step)
        row = first + lax.broadcasted_iota(jnp.int32, (step, LANES), 0)
        for group in range(width // LANES):
            value = src[pl.ds(first, step), group * LANES : (group + 1) * LANES].astype(F32)
            dst[pl.ds(start + first, step), group, :] = jnp.where(row < limit, value, 0.0)
        return carry

    lax.fori_loop(0, rows // step, body, 0)


def spread_small(src, dst, start):
    rows, width = src.shape
    for group in range(width // LANES):
        dst[start : start + rows, group, :] = src[:, group * LANES : (group + 1) * LANES]


def short_block(ref, taps, base, reach, first):
    window = [ref[first + PAD - reach + 1 + i] for i in range(UNROLL + reach - 1)]
    total = [None] * UNROLL
    for offset in range(reach):
        weight = taps[base + offset]
        for i in range(UNROLL):
            term = weight * window[i + reach - 1 - offset]
            total[i] = term if total[i] is None else total[i] + term
    return total


def kernel(
    early, shifts,
    tenant_ref, valid_ref, bias_ref, q_hbm, k_hbm, v_hbm, taps_hbm, residue_hbm, rate_hbm, gain_hbm,
    proj_hbm, weight_hbm, out_ref,
    q_in, k_in, v_in, taps_in, residue_in, rate_in, gain_in, proj_in, weight_in,
    q_rows, k_rows, v_rows, driven_rows, partial_rows, query_rows, mixed, gated,
    taps, decay, scale, grown, halo, ends, incoming, maps, sums, arrived,
    local_sem, halo_send, halo_recv, state_send, state_recv, sum_send, sum_recv,
):
    rows, width = gated.shape
    groups = width // LANES
    reach = taps_in.shape[1]
    modes = rate_in.shape[0]
    spans = tenant_ref.shape[0]
    span = rows // spans
    rank = proj_in.shape[1]
    blocks = rows // UNROLL
    index, count = lax.axis_index("seq"), lax.axis_size("seq")
    place, places = lax.axis_index("ch"), lax.axis_size("ch")
    limit = valid_ref[0] - index * rows

    def remote(src, dst, send, recv, seq, ch):
        return pltpu.make_async_remote_copy(
            src_ref=src, dst_ref=dst, send_sem=send, recv_sem=recv,
            device_id=(seq, ch), device_id_type=pl.DeviceIdType.MESH,
        )

    barrier = pltpu.get_barrier_semaphore()
    steps = sorted({step for group in shifts for step in group})

    def greet(seq, ch):
        pl.semaphore_signal(
            barrier, inc=1, device_id=(seq, ch), device_id_type=pl.DeviceIdType.MESH
        )

    for step in steps:
        pl.when(index + step < count)(lambda step=step: greet(index + step, place))
        pl.when(index >= step)(lambda step=step: greet(index - step, place))
    for offset in range(1, places):
        greet(index, lax.rem(place + offset, places))

    pairs = (
        (k_hbm, k_in), (v_hbm, v_in), (taps_hbm, taps_in), (residue_hbm, residue_in),
        (rate_hbm, rate_in), (gain_hbm, gain_in), (q_hbm, q_in), (proj_hbm, proj_in),
        (weight_hbm, weight_in),
    )
    loads = [
        pltpu.make_async_copy(src, dst, local_sem.at[i]) for i, (src, dst) in enumerate(pairs)
    ]
    for load in loads:
        load.start()
    loads[0].wait()
    spread(k_in, k_rows, PAD, limit)

    peers = places - 1
    for step in steps:
        peers = peers + (index + step < count).astype(jnp.int32)
        peers = peers + (index >= step).astype(jnp.int32)
    pl.semaphore_wait(barrier, peers)

    halos = [
        remote(
            src.at[pl.ds(rows - HALO, HALO)], halo.at[i], halo_send.at[i], halo_recv.at[i],
            index + 1, place,
        )
        for i, src in enumerate((q_hbm, k_hbm, v_hbm))
    ]

    @pl.when(index + 1 < count)
    def _():
        for copy in halos:
            copy.start()

    loads[1].wait()
    spread(v_in, v_rows, PAD, limit)
    for load in loads[2:6]:
        load.wait()
    for i in range(3):
        spread_small(taps_in.at[i], taps, i * reach)
    spread_small(rate_in, grown, 0)
    spread_small(residue_in, scale, 0)
    scale[...] = scale[...] * jnp.sqrt(2.0 * grown[...])
    decay[...] = jnp.exp(-grown[...])

    def drive(first, states):
        keyed = short_block(k_rows, taps, reach, reach, first)
        valued = short_block(v_rows, taps, 2 * reach, reach, first)
        driven = [x * y for x, y in zip(keyed, valued)]
        for i in range(UNROLL):
            driven_rows[first + i] = driven[i]
        after = []
        for n in range(modes):
            d, state = decay[n], states[n]
            for i in range(UNROLL):
                state = driven[i] if state is None else d * state + driven[i]
            after.append(state)
        return tuple(after)

    zeros = (jnp.zeros((groups, LANES), F32),) * modes
    states = lax.fori_loop(1, blocks, lambda b, c: drive(b * UNROLL, c), zeros)
    for n in range(modes):
        ends[0, n] = states[n]

    pl.when(index >= 1)(lambda: [copy.wait_recv() for copy in halos] and None)

    @pl.when(index == 0)
    def _():
        halo[...] = jnp.zeros_like(halo)

    for i, dst in enumerate((q_rows, k_rows, v_rows)):
        row = lax.broadcasted_iota(jnp.int32, (PAD, LANES), 0) - PAD
        for group in range(groups):
            piece = halo[i, :, group * LANES : (group + 1) * LANES].astype(F32)[HALO - PAD :]
            dst[0:PAD, group, :] = jnp.where(row < limit, piece, 0.0)
    states = drive(0, (None,) * modes)
    for n in range(modes):
        ends[0, n] = ends[0, n] + jnp.exp(-float(rows - UNROLL) * grown[n]) * states[n]

    slot = 0
    rounds = []
    for stage, group in enumerate(shifts):
        copies = []
        for step in group:
            copies.append((step, slot, remote(
                ends.at[stage], incoming.at[slot], state_send.at[slot], state_recv.at[slot],
                index + step, place,
            )))
            slot += 1
        rounds.append(copies)

    def send(stage):
        for step, _, copy in rounds[stage]:
            pl.when(index + step < count)(copy.start)

    send(0)
    loads[6].wait()
    spread(q_in, q_rows, PAD, limit)
    gain = gain_in[...]

    def scan(gate, block, states):
        first = block * UNROLL
        driven = [driven_rows[first + i] for i in range(UNROLL)]
        total = [gain * x for x in driven]
        after = []
        for n in range(modes):
            state, d, a = states[n], decay[n], scale[n]
            for i in range(UNROLL):
                state = d * state + driven[i]
                total[i] = total[i] + a * state
            after.append(state)
        query = short_block(q_rows, taps, 0, reach, first)
        for i in range(UNROLL):
            if gate:
                mixed[first + i] = query[i] * total[i]
            else:
                partial_rows[first + i] = total[i]
                query_rows[first + i] = query[i]
        return tuple(after)

    cut = early * span // UNROLL
    states = zeros
    done = 0
    for stage, copies in enumerate(rounds):
        stop = cut * (stage + 1) // len(rounds)
        states = lax.fori_loop(done, stop, functools.partial(scan, False), states)
        done = stop
        first_round = stage == 0
        if first_round:
            ends[1] = jnp.zeros((modes, groups, LANES), F32)
        else:
            ends[stage + 1] = ends[stage]
        covered = 0 if first_round else copies[0][0]
        for step, where, copy in copies:
            factor = float((step - 1 if first_round else covered) * rows)

            @pl.when(index >= step)
            def _():
                copy.wait_recv()
                ends[stage + 1] = ends[stage + 1] + jnp.exp(-factor * grown[...]) * incoming[where]

        if stage + 1 < len(rounds):
            send(stage + 1)

    last = len(rounds)
    if cut < blocks:
        states = tuple(
            states[n] + jnp.exp(-float(cut * UNROLL) * grown[n]) * ends[last, n]
            for n in range(modes)
        )

    def correct(block, states):
        first = block * UNROLL
        total = [partial_rows[first + i] for i in range(UNROLL)]
        after = []
        for n in range(modes):
            state, d = states[n], decay[n]
            for i in range(UNROLL):
                total[i] = total[i] + state
                state = state * d
            after.append(state)
        for i in range(UNROLL):
            mixed[first + i] = total[i] * query_rows[first + i]
        return tuple(after)

    def gather(block, carry):
        first = pl.multiple_of(block * 64, 64)
        for group in range(groups):
            gated[pl.ds(first, 64), group * LANES : (group + 1) * LANES] = mixed[
                pl.ds(first, 64), group, :
            ]
        return carry

    loads[7].wait()
    loads[8].wait()
    order = list(range(early, spans)) + list(range(early))
    sends = {}
    per = span // UNROLL
    for s in order:
        if s == 0:
            states = tuple(scale[n] * decay[n] * ends[last, n] for n in range(modes))
        body = functools.partial(scan, True) if s >= early else correct
        states = lax.fori_loop(s * per, (s + 1) * per, body, states)
        lax.fori_loop(s * span // 64, (s + 1) * span // 64, gather, 0)
        tenant = tenant_ref[s]
        maps[0:rank, :] = proj_in[tenant].astype(F32)
        maps[rank : 2 * rank, :] = weight_in[tenant].astype(F32)
        both = maps[...].astype(BF16)
        value = gated[s * span : (s + 1) * span, :]
        high = value.astype(BF16)
        low = (value - high.astype(F32)).astype(BF16)
        dims = (((1,), (1,)), ((), ()))
        sums[s] = lax.dot_general(
            both, high, dims, preferred_element_type=F32
        ) + lax.dot_general(both, low, dims, preferred_element_type=F32)
        sends[s] = [
            remote(
                sums.at[s], arrived.at[offset - 1, s], sum_send.at[offset - 1, s],
                sum_recv.at[offset - 1, s], index, lax.rem(place + offset, places),
            )
            for offset in range(1, places)
        ]
        for copy in sends[s]:
            copy.start()

    line = lax.broadcasted_iota(jnp.int32, (2 * rank, span), 0)
    for s in order:
        tenant = tenant_ref[s]
        maps[0:rank, :] = proj_in[tenant].astype(F32)
        maps[rank : 2 * rank, :] = proj_in[tenant].astype(F32)
        totals = sums[s]
        for offset in range(1, places):
            sends[s][offset - 1].wait_recv()
            totals = totals + arrived[offset - 1, s]
        bias = jnp.zeros((2 * rank, span), F32)
        for r in range(rank):
            bias = jnp.where(line % rank == r, bias_ref[tenant, r], bias)
        change = pltpu.roll(totals, rank, 0) - totals
        delta = jnp.where(line < rank, change, -change) + bias
        high = delta.astype(BF16).astype(F32)
        parts = jnp.where(line < rank, high, delta - high).astype(BF16)
        edit = lax.dot_general(
            parts, maps[...].astype(BF16), (((0,), (0,)), ((), ())), preferred_element_type=F32
        )
        row = s * span + lax.broadcasted_iota(jnp.int32, (span, width), 0)
        value = gated[s * span : (s + 1) * span, :] + edit
        out_ref[s * span : (s + 1) * span, :] = jnp.where(row < limit, value, 0.0).astype(BF16)

    @pl.when(index + 1 < count)
    def _():
        for copy in halos:
            copy.wait_send()

    for copies in rounds:
        for step, _, copy in copies:
            pl.when(index + step < count)(copy.wait_send)
    for s in order:
        for copy in sends[s]:
            copy.wait_send()


VMEM = pl.BlockSpec(memory_space=pltpu.VMEM)
SMEM = pl.BlockSpec(memory_space=pltpu.SMEM)
HBM = pl.BlockSpec(memory_space=pl.ANY)


def local(
    q_in, k_in, v_in, conv_weight, mode_residue, decay_rate, skip_gain, tenant_ids, valid_length,
    reft_proj, reft_weight, reft_bias,
):
    rows, width = q_in.shape
    groups = width // LANES
    modes = decay_rate.shape[0]
    reach = conv_weight.shape[1]
    rank = reft_bias.shape[1]
    spans = tenant_ids.shape[0]
    count, places = lax.axis_size("seq"), lax.axis_size("ch")
    shifts = [(1, 2)]
    while 2 ** len(shifts) < count:
        shifts.append((2 ** len(shifts),))
    slots = len(shifts) + 1
    gain = skip_gain.reshape(groups, LANES)
    args = (q_in, k_in, v_in, conv_weight, mode_residue, decay_rate, gain, reft_proj, reft_weight)
    tall = pltpu.VMEM((rows + PAD, groups, LANES), F32)
    cube = pltpu.VMEM((rows, groups, LANES), F32)
    small = pltpu.VMEM((modes, groups, LANES), F32)
    dma = pltpu.SemaphoreType.DMA
    return pl.pallas_call(
        functools.partial(kernel, spans - 1, tuple(shifts)),
        out_shape=jax.ShapeDtypeStruct((rows, width), BF16),
        in_specs=[SMEM] * 3 + [HBM] * 9,
        out_specs=VMEM,
        scratch_shapes=[pltpu.VMEM(x.shape, x.dtype) for x in args]
        + [tall, tall, tall, cube, cube, cube, cube, pltpu.VMEM((rows, width), F32)]
        + [pltpu.VMEM((3 * reach, groups, LANES), F32), small, small, small]
        + [
            pltpu.VMEM((3, HALO, width), BF16),
            pltpu.VMEM((slots, modes, groups, LANES), F32),
            pltpu.VMEM((slots, modes, groups, LANES), F32),
            pltpu.VMEM((2 * rank, width), F32),
            pltpu.VMEM((spans, 2 * rank, rows // spans), F32),
            pltpu.VMEM((places - 1, spans, 2 * rank, rows // spans), F32),
        ]
        + [dma((len(args),)), dma((3,)), dma((3,)), dma((slots,)), dma((slots,))]
        + [dma((places - 1, spans)), dma((places - 1, spans))],
        compiler_params=pltpu.CompilerParams(
            collective_id=0, has_side_effects=True, vmem_limit_bytes=56 * 2**20
        ),
    )(tenant_ids, valid_length, reft_bias, *args)


def solution(mesh):
    return jax.shard_map(
        local,
        mesh=mesh,
        in_specs=(
            P("seq", "ch"),
            P("seq", "ch"),
            P("seq", "ch"),
            P(None, None, "ch"),
            P(None, "ch"),
            P(None, "ch"),
            P("ch"),
            P("seq"),
            P(),
            P(None, None, "ch"),
            P(None, None, "ch"),
            P(),
        ),
        out_specs=P("seq", "ch"),
        check_vma=False,
    )
```

time: 80 us -> 34.6 us (0.43)
  the two profiles are of different devices: /device:TPU:0 before, /device:TPU:19 now
where the time goes in v1:
time: 34.6 us; the launch traced here: 34.3 us
  Pallas kernels  30.7 us (89%)
  local copies, waits for them, and re-layouts  2.95 us (9%)
  between operations  0.68 us (2%)
    pallas_call x1, Pallas kernels, local(): pl.pallas_call(functools.partial(kernel, spans - 1, tuple(shifts)), out_s...  30.7 us
    unnamed x4, local copies, waits for them, and re-layouts  2.95 us

profile of v1, /device:TPU:19, one launch (start us, length us, event | category | flops | bytes accessed | tf_op | source)
XLA Modules:
  0.0 34.3 jit_solution(16544892611098982828)
XLA Ops:
  0.0 0.0 copy-start
  0.7 0.0 copy-done
  0.7 0.7 %copy.13.bias_ref = f32[8,4]{1,0:T(8,128)} copy(f32[8,4]{0,1:T(4,128)S(1)} %copy-done) | data formatting | bytes 256 | tf_op args[11]
  1.4 30.7 %shard_map.118 = bf16[512,1024]{1,0:T(8,128)(2,1)} custom-call(s32[4]{0:T(128)} %tenant_ref.1, s32[1]{0:T(128)S(6)} %copy.15.valid_ref, f32[8,4]{1,0:T(8,128)} %copy.13.bias_ref, bf16[512,1024]{1,0:T(8,128)(2,1)} %q_hbm.1, bf16[512,1024]{1,0:T(8,128)(2,1)} %k_hbm.1, bf16[512,1024]{1,0:T(8,128)(2,1)} %v_hbm.1, f32[3,7,1024]{2,1,0:T(8,128)} %taps_hbm.1, ...), custom_call_target="tpu_custom_call" | custom-call | tf_op jit(solution)/shard_map/pallas_call | solution.py:356
  32.1 2.3 %copy.16 = bf16[512,1024]{1,0:T(8,128)(2,1)} copy(bf16[512,1024]{1,0:T(8,128)(2,1)} %shard_map.118) | data formatting | bytes 2097152
Async XLA Ops:
  0.0 0.7 %copy-start = (f32[8,4]{0,1:T(4,128)S(1)}, f32[8,4]{0,1:T(4,128)}, u32[]{:S(2)}) copy-start(f32[8,4]{0,1:T(4,128)} %param.23) | copy-start | bytes 388

commit v2 on v1

--- a/solution.py
+++ b/solution.py
@@ -50,11 +50,11 @@
 def kernel(
     early, shifts,
     tenant_ref, valid_ref, bias_ref, q_hbm, k_hbm, v_hbm, taps_hbm, residue_hbm, rate_hbm, gain_hbm,
-    proj_hbm, weight_hbm, out_ref,
+    proj_hbm, weight_hbm, out_hbm,
     q_in, k_in, v_in, taps_in, residue_in, rate_in, gain_in, proj_in, weight_in,
     q_rows, k_rows, v_rows, driven_rows, partial_rows, query_rows, mixed, gated,
     taps, decay, scale, grown, halo, ends, incoming, maps, sums, arrived,
-    local_sem, halo_send, halo_recv, state_send, state_recv, sum_send, sum_recv,
+    local_sem, halo_send, halo_recv, state_send, state_recv, sum_send, sum_recv, out_ref, out_sem,
 ):
     rows, width = gated.shape
     groups = width // LANES
@@ -292,6 +292,7 @@
             copy.start()
 
     line = lax.broadcasted_iota(jnp.int32, (2 * rank, span), 0)
+    stores = []
     for s in order:
         tenant = tenant_ref[s]
         maps[0:rank, :] = proj_in[tenant].astype(F32)
@@ -302,7 +303,7 @@
             totals = totals + arrived[offset - 1, s]
         bias = jnp.zeros((2 * rank, span), F32)
         for r in range(rank):
-            bias = jnp.where(line % rank == r, bias_ref[tenant, r], bias)
+            bias = jnp.where(line % rank == r, bias_ref[r, tenant], bias)
         change = pltpu.roll(totals, rank, 0) - totals
         delta = jnp.where(line < rank, change, -change) + bias
         high = delta.astype(BF16).astype(F32)
@@ -313,6 +314,9 @@
         row = s * span + lax.broadcasted_iota(jnp.int32, (span, width), 0)
         value = gated[s * span : (s + 1) * span, :] + edit
         out_ref[s * span : (s + 1) * span, :] = jnp.where(row < limit, value, 0.0).astype(BF16)
+        part = pl.ds(s * span, span)
+        stores.append(pltpu.make_async_copy(out_ref.at[part], out_hbm.at[part], out_sem.at[s]))
+        stores[-1].start()
 
     @pl.when(index + 1 < count)
     def _():
@@ -325,11 +329,13 @@
     for s in order:
         for copy in sends[s]:
             copy.wait_send()
+    for store in stores:
+        store.wait()
 
 
 VMEM = pl.BlockSpec(memory_space=pltpu.VMEM)
 SMEM = pl.BlockSpec(memory_space=pltpu.SMEM)
-HBM = pl.BlockSpec(memory_space=pl.ANY)
+HBM = pl.BlockSpec(memory_space=pltpu.HBM)
 
 
 def local(
@@ -357,7 +363,7 @@
         functools.partial(kernel, spans - 1, tuple(shifts)),
         out_shape=jax.ShapeDtypeStruct((rows, width), BF16),
         in_specs=[SMEM] * 3 + [HBM] * 9,
-        out_specs=VMEM,
+        out_specs=HBM,
         scratch_shapes=[pltpu.VMEM(x.shape, x.dtype) for x in args]
         + [tall, tall, tall, cube, cube, cube, cube, pltpu.VMEM((rows, width), F32)]
         + [pltpu.VMEM((3 * reach, groups, LANES), F32), small, small, small]
@@ -370,11 +376,12 @@
             pltpu.VMEM((places - 1, spans, 2 * rank, rows // spans), F32),
         ]
         + [dma((len(args),)), dma((3,)), dma((3,)), dma((slots,)), dma((slots,))]
-        + [dma((places - 1, spans)), dma((places - 1, spans))],
+        + [dma((places - 1, spans)), dma((places - 1, spans))]
+        + [pltpu.VMEM((rows, width), BF16), dma((spans,))],
         compiler_params=pltpu.CompilerParams(
-            collective_id=0, has_side_effects=True, vmem_limit_bytes=56 * 2**20
+            collective_id=0, has_side_effects=True, vmem_limit_bytes=60 * 2**20
         ),
-    )(tenant_ids, valid_length, reft_bias, *args)
+    )(tenant_ids, valid_length, reft_bias.T, *args)
 
 
 def solution(mesh):

time: 34.6 us -> 33.5 us (0.968)
  local copies, waits for them, and re-layouts: 2.95 us -> 2.26 us
    unnamed x4 -> x1, local copies, waits for them, and re-layouts: 2.95 us -> 2.26 us
where the time goes in v2:
time: 33.5 us; the launch traced here: 33.4 us
  Pallas kernels  30.4 us (91%)
  local copies, waits for them, and re-layouts  2.26 us (7%)
  between operations  0.66 us (2%)
    pallas_call x1, Pallas kernels, local(): pl.pallas_call(functools.partial(kernel, spans - 1, tuple(shifts)), out_s...  30.4 us
    unnamed x1, local copies, waits for them, and re-layouts  2.26 us

profile of v2, /device:TPU:19, one launch (start us, length us, event | category | flops | bytes accessed | tf_op | source)
XLA Modules:
  0.0 33.4 jit_solution(1817756352852006108)
XLA Ops:
  0.7 30.4 %shard_map.118 = bf16[512,1024]{1,0:T(8,128)(2,1)} custom-call(s32[4]{0:T(128)} %tenant_ref.1, s32[1]{0:T(128)S(6)} %copy.14.valid_ref, f32[4,8]{1,0:T(4,128)} %bitcast.3, bf16[512,1024]{1,0:T(8,128)(2,1)} %q_hbm.1, bf16[512,1024]{1,0:T(8,128)(2,1)} %k_hbm.1, bf16[512,1024]{1,0:T(8,128)(2,1)} %v_hbm.1, f32[3,7,1024]{2,1,0:T(8,128)} %taps_hbm.1, ...), custom_call_target="tpu_custom_call" | custom-call | tf_op jit(solution)/shard_map/pallas_call | solution.py:362
  31.1 2.3 %copy.15 = bf16[512,1024]{1,0:T(8,128)(2,1)} copy(bf16[512,1024]{1,0:T(8,128)(2,1)} %shard_map.118) | data formatting | bytes 2097152

commit v3 on v2

--- a/solution.py
+++ b/solution.py
@@ -8,7 +8,7 @@
 from jax.sharding import PartitionSpec as P
 
 LANES = 128
-UNROLL = 8
+UNROLL = 16
 PAD = 8
 HALO = 16
 F32 = jnp.float32

time: 33.5 us -> 33.2 us (level)
    pallas_call x1, Pallas kernels: 30.4 us -> 30.1 us  [local(): pl.pallas_call(functools.partial(kernel, spans - 1, tuple(shifts)), out_s...]
where the time goes in v3:
time: 33.2 us; the launch traced here: 33 us
  Pallas kernels  30.1 us (91%)
  local copies, waits for them, and re-layouts  2.26 us (7%)
  between operations  0.66 us (2%)
    pallas_call x1, Pallas kernels, local(): pl.pallas_call(functools.partial(kernel, spans - 1, tuple(shifts)), out_s...  30.1 us
    unnamed x1, local copies, waits for them, and re-layouts  2.26 us

profile of v3, /device:TPU:19, one launch (start us, length us, event | category | flops | bytes accessed | tf_op | source)
XLA Modules:
  0.0 33.0 jit_solution(9276150824781233913)
XLA Ops:
  0.7 30.1 %shard_map.118 = bf16[512,1024]{1,0:T(8,128)(2,1)} custom-call(s32[4]{0:T(128)} %tenant_ref.1, s32[1]{0:T(128)S(6)} %copy.14.valid_ref, f32[4,8]{1,0:T(4,128)} %bitcast.3, bf16[512,1024]{1,0:T(8,128)(2,1)} %q_hbm.1, bf16[512,1024]{1,0:T(8,128)(2,1)} %k_hbm.1, bf16[512,1024]{1,0:T(8,128)(2,1)} %v_hbm.1, f32[3,7,1024]{2,1,0:T(8,128)} %taps_hbm.1, ...), custom_call_target="tpu_custom_call" | custom-call | tf_op jit(solution)/shard_map/pallas_call | solution.py:362
  30.7 2.3 %copy.15 = bf16[512,1024]{1,0:T(8,128)(2,1)} copy(bf16[512,1024]{1,0:T(8,128)(2,1)} %shard_map.118) | data formatting | bytes 2097152
